TPU v7x, 32 devices: a whole 2x2x4 slice. The times are simulated.
32 devices in a mesh: tab: 8 (over y, x, core), blk: 4 (over z).
Axes of the slice: x: 2, y: 2, z: 4, core: 2. Of those that a mesh axis runs over, the one named last changes fastest.
Arguments:
- cells: bfloat16 [8, 1024, 3, 512], P('tab', 'blk'), may hold values from -6 to 6
- missing: int32 [8, 1024, 3], P('tab', 'blk'), may hold values 0 or 1
- context: int32 [8, 1024], P('tab', 'blk'), may hold values from 0 to 1, as said below
- cotangent: bfloat16 [8, 1024, 3, 512], P('tab', 'blk'), may hold values from -6 to 6
- miss_embed: bfloat16 [512], replicated, may hold values from -4 to 4
- norm1_gain: bfloat16 [512], replicated, may hold values from 0.5 to 1.5
- norm1_shift: bfloat16 [512], replicated, may hold values from -2 to 2
- feat_qkv: bfloat16 [512, 1536], replicated, may hold values from -0.375 to 0.375
- feat_out: bfloat16 [512, 512], replicated, may hold values from -0.25 to 0.25
- norm2_gain: bfloat16 [512], replicated, may hold values from 0.5 to 1.5
- norm2_shift: bfloat16 [512], replicated, may hold values from -2 to 2
- row_qkv: bfloat16 [512, 1536], replicated, may hold values from -0.375 to 0.375
- row_out: bfloat16 [512, 512], replicated, may hold values from -2 to 2
- norm3_gain: bfloat16 [512], replicated, may hold values from 0.5 to 1.5
- norm3_shift: bfloat16 [512], replicated, may hold values from -2 to 2
- ff_in: bfloat16 [512, 2048], replicated, may hold values from -0.25 to 0.25
- ff_in_bias: bfloat16 [2048], replicated, may hold values from -2 to 2
- ff_out: bfloat16 [2048, 512], replicated, may hold values from -0.1875 to 0.1875
- ff_out_bias: bfloat16 [512], replicated, may hold values from -2 to 2
Outputs:
- activations: bfloat16 [8, 1024, 3, 512], P('tab', 'blk')
- input_grad: float32 [8, 1024, 3, 512], P('tab', 'blk')
- grad_miss_embed: float32 [512], replicated
- grad_norm1_gain: float32 [512], replicated
- grad_norm1_shift: float32 [512], replicated
- grad_feat_qkv: float32 [512, 1536], replicated
- grad_feat_out: float32 [512, 512], replicated
- grad_norm2_gain: float32 [512], replicated
- grad_norm2_shift: float32 [512], replicated
- grad_row_qkv: float32 [512, 1536], replicated
- grad_row_out: float32 [512, 512], replicated
- grad_norm3_gain: float32 [512], replicated
- grad_norm3_shift: float32 [512], replicated
- grad_ff_in: float32 [512, 2048], replicated
- grad_ff_in_bias: float32 [2048], replicated
- grad_ff_out: float32 [2048, 512], replicated
- grad_ff_out_bias: float32 [512], replicated
Inputs may be any that keep to these rules, and one draw needn't show every extreme that they name: Row 0 of every table is a context row.
All inputs are finite; a program needn't handle non-finite values. No bound on the sum of `missing` on one device may be relied on, other than what follows from the above.
Results may differ from a plain program's by a relative error of at most 0.023.
The roundings to bfloat16 on the way count: a program that leaves them out, or rounds other values in their place, can miss the bound.
Values may be sent and summed in bfloat16 or wider, within the bound.
A program may use at most 128 MiB of HBM per device.

v0:
```python
import math

import jax
import jax.numpy as jnp
from jax import lax
from jax.sharding import PartitionSpec as P

HEADS = 4
HEAD = 128


epsilon = 1e-05
masked_score = -1e30


def normalize(inputs, scales, shifts):
    center = inputs - jnp.mean(inputs, axis=-1, keepdims=True)
    spread = jnp.mean(center * center, axis=-1, keepdims=True)
    return center * lax.rsqrt(spread + epsilon) * scales + shifts


def norm_back(inputs, scales, shifts, grad_out):
    result, pullback = jax.vjp(normalize, inputs, scales, shifts)
    return pullback(grad_out)


def matmul_plain(left, right):
    return jnp.dot(left, right, preferred_element_type=jnp.float32)


def matmul_left_t(left, right):
    return lax.dot_general(
        left, right, (((0,), (0,)), ((), ())), preferred_element_type=jnp.float32
    )


def matmul_right_t(left, right):
    return lax.dot_general(
        left, right, (((1,), (1,)), ((), ())), preferred_element_type=jnp.float32
    )


def per_device(
    cells,
    missing,
    context,
    cotangent,
    miss_embed,
    norm1_gain,
    norm1_shift,
    feat_qkv,
    feat_out,
    norm2_gain,
    norm2_shift,
    row_qkv,
    row_out,
    norm3_gain,
    norm3_shift,
    ff_in,
    ff_in_bias,
    ff_out,
    ff_out_bias,
):
    rows_dev = cells.shape[1]
    columns = cells.shape[2]
    model_width = cells.shape[3]
    head_count = HEADS
    head_size = HEAD
    cell_count = rows_dev * columns
    score_scale = 1.0 / math.sqrt(HEAD)
    f32 = jnp.float32
    bf16 = jnp.bfloat16
    gain_one = norm1_gain.astype(f32)
    shift_one = norm1_shift.astype(f32)
    gain_two = norm2_gain.astype(f32)
    shift_two = norm2_shift.astype(f32)
    gain_three = norm3_gain.astype(f32)
    shift_three = norm3_shift.astype(f32)
    absent = missing.reshape(cell_count, 1) > 0
    base_cells = jnp.where(
        absent, miss_embed.astype(f32)[None, :], cells.reshape(cell_count, model_width).astype(f32)
    )
    normed_one = normalize(base_cells, gain_one, shift_one).astype(bf16)
    packed_one = (
        matmul_plain(normed_one, feat_qkv)
        .astype(bf16)
        .reshape(rows_dev, columns, 3, head_count, head_size)
    )
    feat_queries = packed_one[:, :, 0]
    feat_keys = packed_one[:, :, 1]
    feat_values = packed_one[:, :, 2]
    feat_scores = (
        jnp.einsum("rihe,rjhe->rhij", feat_queries, feat_keys, preferred_element_type=f32)
        * score_scale
    )
    feat_probs = jax.nn.softmax(feat_scores, axis=-1)
    feat_probs_low = feat_probs.astype(bf16)
    feat_attended = (
        jnp.einsum("rhij,rjhe->rihe", feat_probs_low, feat_values, preferred_element_type=f32)
        .astype(bf16)
        .reshape(cell_count, model_width)
    )
    after_feat = base_cells + matmul_plain(feat_attended, feat_out)
    normed_two = normalize(after_feat, gain_two, shift_two).astype(bf16)
    packed_two = (
        matmul_plain(normed_two, row_qkv)
        .astype(bf16)
        .reshape(rows_dev, columns, 3, head_count, head_size)
    )
    row_queries = packed_two[:, :, 0]
    row_keys = packed_two[:, :, 1]
    row_values = packed_two[:, :, 2]
    row_marks = context.reshape(rows_dev).astype(bf16)
    running_max = jnp.full((columns, head_count, rows_dev, 1), masked_score, f32)
    keys_piece = lax.all_gather(row_keys, "blk", axis=0, tiled=True)
    values_piece = lax.all_gather(row_values, "blk", axis=0, tiled=True)
    marks_piece = lax.all_gather(row_marks, "blk", axis=0, tiled=True)
    usable = marks_piece > 0.5
    piece_scores = (
        jnp.einsum("iche,jche->chij", row_queries, keys_piece, preferred_element_type=f32)
        * score_scale
    )
    piece_scores = jnp.where(usable, piece_scores, masked_score)
    new_max = jnp.maximum(running_max, jnp.max(piece_scores, axis=-1, keepdims=True))
    exponent = jnp.where(usable, jnp.exp(piece_scores - new_max), 0.0)
    row_total = jnp.sum(exponent, axis=-1, keepdims=True)
    accum = jnp.einsum(
        "chij,jche->chie", exponent.astype(bf16), values_piece, preferred_element_type=f32
    )
    running_max, row_total, accum = (new_max, row_total, accum)
    log_total = running_max + jnp.log(row_total)
    row_attended = jnp.transpose(accum / row_total, (2, 0, 1, 3))
    row_attended_low = row_attended.astype(bf16).reshape(cell_count, model_width)
    after_rows = after_feat + matmul_plain(row_attended_low, row_out)
    normed_three = normalize(after_rows, gain_three, shift_three).astype(bf16)
    inner_act = matmul_plain(normed_three, ff_in) + ff_in_bias.astype(f32)
    hidden = jax.nn.gelu(inner_act).astype(bf16)
    final_sum = after_rows + matmul_plain(hidden, ff_out) + ff_out_bias.astype(f32)
    activations = final_sum.astype(bf16).reshape(cells.shape)
    grad_three = cotangent.reshape(cell_count, model_width).astype(f32)
    branch_three = grad_three.astype(bf16)
    g_ff_out_bias = jnp.sum(branch_three.astype(f32), axis=0)
    g_ff_out = matmul_left_t(hidden, branch_three)
    grad_hidden = matmul_right_t(branch_three, ff_out)
    gelu_result, gelu_pull = jax.vjp(jax.nn.gelu, inner_act)
    grad_inner = gelu_pull(grad_hidden)[0].astype(bf16)
    g_ff_in_bias = jnp.sum(grad_inner.astype(f32), axis=0)
    g_ff_in = matmul_left_t(normed_three, grad_inner)
    grad_normed_three = matmul_right_t(grad_inner, ff_in)
    input_part, g_gain_three, g_shift_three = norm_back(
        after_rows, gain_three, shift_three, grad_normed_three
    )
    grad_two = grad_three + input_part
    branch_two = grad_two.astype(bf16)
    g_row_out = matmul_left_t(row_attended_low, branch_two)
    grad_attended = (
        matmul_right_t(branch_two, row_out)
        .astype(bf16)
        .reshape(rows_dev, columns, head_count, head_size)
    )
    grad_dot = jnp.transpose(jnp.sum(grad_attended.astype(f32) * row_attended, axis=-1), (1, 2, 0))[
        ..., None
    ]
    keys_back, values_back, marks_back = (
        lax.all_gather(row_keys, "blk", axis=0, tiled=True),
        lax.all_gather(row_values, "blk", axis=0, tiled=True),
        lax.all_gather(row_marks, "blk", axis=0, tiled=True),
    )
    usable_back = marks_back > 0.5
    back_scores = (
        jnp.einsum("iche,jche->chij", row_queries, keys_back, preferred_element_type=f32)
        * score_scale
    )
    back_probs = jnp.where(usable_back, jnp.exp(back_scores - log_total), 0.0)
    grad_probs = jnp.einsum(
        "iche,jche->chij", grad_attended, values_back, preferred_element_type=f32
    )
    grad_scores = (back_probs * (grad_probs - grad_dot)).astype(bf16)
    grad_queries = (
        jnp.einsum("chij,jche->iche", grad_scores, keys_back, preferred_element_type=f32)
        * score_scale
    )
    back_probs_low = back_probs.astype(bf16)
    grad_keys_part = (
        jnp.einsum("chij,iche->jche", grad_scores, row_queries, preferred_element_type=f32)
        * score_scale
    )
    grad_values_part = jnp.einsum(
        "chij,iche->jche", back_probs_low, grad_attended, preferred_element_type=f32
    )
    key_value_sum = lax.psum_scatter(
        jnp.concatenate(
            [
                grad_keys_part.reshape(rows_dev * lax.axis_size("blk"), columns, model_width),
                grad_values_part.reshape(rows_dev * lax.axis_size("blk"), columns, model_width),
            ],
            axis=-1,
        ).astype(jnp.bfloat16),
        "blk",
        scatter_dimension=0,
        tiled=True,
    ).astype(jnp.float32)
    grad_packed_two = (
        jnp.concatenate(
            [grad_queries.reshape(rows_dev, columns, model_width), key_value_sum], axis=-1
        )
        .astype(bf16)
        .reshape(cell_count, 3 * model_width)
    )
    g_row_qkv = matmul_left_t(normed_two, grad_packed_two)
    grad_normed_two = matmul_right_t(grad_packed_two, row_qkv)
    input_part, g_gain_two, g_shift_two = norm_back(
        after_feat, gain_two, shift_two, grad_normed_two
    )
    grad_one = grad_two + input_part
    branch_one = grad_one.astype(bf16)
    g_feat_out = matmul_left_t(feat_attended, branch_one)
    grad_feat_att = (
        matmul_right_t(branch_one, feat_out)
        .astype(bf16)
        .reshape(rows_dev, columns, head_count, head_size)
    )
    grad_feat_probs = jnp.einsum(
        "rihe,rjhe->rhij", grad_feat_att, feat_values, preferred_element_type=f32
    )
    grad_feat_scores = (
        feat_probs
        * (grad_feat_probs - jnp.sum(feat_probs * grad_feat_probs, axis=-1, keepdims=True))
    ).astype(bf16)
    grad_feat_queries = (
        jnp.einsum("rhij,rjhe->rihe", grad_feat_scores, feat_keys, preferred_element_type=f32)
        * score_scale
    )
    grad_feat_keys = (
        jnp.einsum("rhij,rihe->rjhe", grad_feat_scores, feat_queries, preferred_element_type=f32)
        * score_scale
    )
    grad_feat_values = jnp.einsum(
        "rhij,rihe->rjhe", feat_probs_low, grad_feat_att, preferred_element_type=f32
    )
    grad_packed_one = jnp.concatenate(
        [
            grad_feat_queries.reshape(cell_count, model_width),
            grad_feat_keys.reshape(cell_count, model_width),
            grad_feat_values.reshape(cell_count, model_width),
        ],
        axis=-1,
    ).astype(bf16)
    g_feat_qkv = matmul_left_t(normed_one, grad_packed_one)
    grad_normed_one = matmul_right_t(grad_packed_one, feat_qkv)
    input_part, g_gain_one, g_shift_one = norm_back(
        base_cells, gain_one, shift_one, grad_normed_one
    )
    grad_base = grad_one + input_part
    g_miss = jnp.sum(jnp.where(absent, grad_base, 0.0), axis=0)
    input_grad = jnp.where(absent, 0.0, grad_base).reshape(cells.shape)
    (
        g_miss,
        g_gain_one,
        g_shift_one,
        g_feat_qkv,
        g_feat_out,
        g_gain_two,
        g_shift_two,
        g_row_qkv,
        g_row_out,
        g_gain_three,
        g_shift_three,
        g_ff_in,
        g_ff_in_bias,
        g_ff_out,
        g_ff_out_bias,
    ) = lax.psum(
        (
            g_miss,
            g_gain_one,
            g_shift_one,
            g_feat_qkv,
            g_feat_out,
            g_gain_two,
            g_shift_two,
            g_row_qkv,
            g_row_out,
            g_gain_three,
            g_shift_three,
            g_ff_in,
            g_ff_in_bias,
            g_ff_out,
            g_ff_out_bias,
        ),
        ("tab", "blk"),
    )
    return (
        activations,
        input_grad,
        g_miss,
        g_gain_one,
        g_shift_one,
        g_feat_qkv,
        g_feat_out,
        g_gain_two,
        g_shift_two,
        g_row_qkv,
        g_row_out,
        g_gain_three,
        g_shift_three,
        g_ff_in,
        g_ff_in_bias,
        g_ff_out,
        g_ff_out_bias,
    )


def solution(mesh):
    placed = (
        P("tab", "blk", None, None),
        P("tab", "blk", None),
        P("tab", "blk"),
        P("tab", "blk", None, None),
        P(),
        P(),
        P(),
        P(),
        P(),
        P(),
        P(),
        P(),
        P(),
        P(),
        P(),
        P(),
        P(),
        P(),
        P(),
    )
    return jax.shard_map(
        per_device,
        mesh=mesh,
        in_specs=placed,
        out_specs=(
            P("tab", "blk", None, None),
            P("tab", "blk", None, None),
            P(),
            P(),
            P(),
            P(),
            P(),
            P(),
            P(),
            P(),
            P(),
            P(),
            P(),
            P(),
            P(),
            P(),
            P(),
        ),
        check_vma=False,
    )
```

profile of v0, /device:TPU:0, one launch (start us, length us, event | category | flops | bytes accessed | tf_op | source)
XLA Modules:
  0.0 899.6 jit_solution(1494741154924084800)
XLA Ops:
  15.3 4.0 reshape.279
  19.3 4.8 convolution_convert_fusion.1
  24.1 5.2 reshape.265
  29.3 3.6 fusion.79
  32.9 6.9 fusion.80
  49.1 5.2 reshape.267
  54.3 3.3 fusion.78
  67.4 12.9 %all-gather = bf16[1,1024]{1,0:T(2,128)(2,1)S(1)} all-gather(bf16[1,256]{1,0:T(2,128)(2,1)S(1)} %convert_element_type.133), channel_id=2, replica_groups=mesh['tab'=8,'blk'=4] {'blk'}, dimensions={1}, use_global_device_ids=true | all-gather | bytes 2560 | tf_op jit(solution)/shard_map/all_gather | solution.py:117
  80.4 44.7 %all-gather.6.cloned.1.call-done = bf16[1024,3,1,4,128]{4,0,3,1,2:T(8,128)(2,1)} async-done(((bf16[256,3,1,4,128]{4,0,3,1,2:T(8,128)(2,1)}), bf16[1024,3,1,4,128]{4,0,3,1,2:T(8,128)(2,1)}) %all-gather.6.cloned.1.call-update) | async-done | bytes 3145744 | tf_op jit(solution)/shard_map/all_gather | solution.py:115
  125.0 3.9 select_reduce_fusion
  128.9 3.5 fusion.2
  133.6 55.6 %all-gather.8.cloned.1.call-done = bf16[1024,3,1,4,128]{0,4,3,1,2:T(8,128)(2,1)} async-done(((bf16[256,3,1,4,128]{0,4,3,1,2:T(8,128)(2,1)}), bf16[1024,3,1,4,128]{0,4,3,1,2:T(8,128)(2,1)}) %all-gather.8.cloned.1.call-update) | async-done | bytes 3145744 | tf_op jit(solution)/shard_map/all_gather | solution.py:116
  189.2 8.4 fusion.82
  202.7 4.8 multiply_convert_fusion.2
  207.4 5.6 convert_reduce_fusion
  224.8 9.1 %fusion.26 = bf16[3,4,128,1024]{3,2,1,0:T(8,128)(2,1)} fusion(bf16[256,3,4,128]{0,3,2,1:T(8,128)(2,1)S(1)} %copy.100, f32[3,4,256,1024]{3,2,1,0:T(8,128)} %copy-done.2, f32[3,4,256]{2,1,0:T(4,128)S(1)} %log_add_fusion, pred[1024]{0:T(1024)(128)(4,1)S(1)} %compare_reduce_fusion), kind=kOutput, calls=%fused_computation.39 | convolution fusion | flops 819462144 | bytes 16528384 | tf_op jit(solution)/shard_map/chij,iche->jche/dot_general | solution.py:188
  233.9 6.8 multiply_convert_fusion
  240.7 3.3 multiply_convert_fusion.1
  244.3 7.6 copy.106
  251.9 7.6 copy.105
  259.5 8.3 pad_maximum_fusion
  269.7 6.7 fusion.40
  283.0 3.9 fusion.84
  286.9 4.1 fusion.72
  291.0 266.0 %all-reduce.6.cloned.1.call-done = bf16[1024,3,1024]{2,1,0:T(4,128)(2,1)} async-done(((bf16[1024,3,1024]{2,1,0:T(4,128)(2,1)}), bf16[1024,3,1024]{2,1,0:T(4,128)(2,1)}) %all-reduce.6.cloned.1.call-update) | async-done | bytes 6291472
  564.7 3.6 multiply_reduce_fusion.3
  577.4 3.3 fusion.37
  595.7 5.2 add_convert_fusion
  604.5 4.0 multiply_reduce_fusion.4
  615.8 41.2 %all-reduce.1 = (f32[512]{0:T(512)}, f32[512]{0:T(512)}, f32[512]{0:T(512)}, f32[512]{0:T(512)}, f32[512]{0:T(512)}, /*index=5*/f32[512]{0:T(512)}, f32[512]{0:T(512)}, f32[2048]{0:T(1024)}, f32[512]{0:T(512)}) all-reduce(f32[512]{0:T(512)S(1)} %get-tuple-element.98, ...), channel_id=1, replica_groups=mesh['tab'=8,'blk'=4] {'tab','blk'}, use_global_device_ids=true, to_apply=%region_20.21 | all-reduce | flops 6144 | bytes 49152 | tf_op jit(solution)/shard_map/psum | solution.py:273
  657.0 220.0 %all-reduce.8.cloned.1.call-done = (f32[512,1536]{1,0:T(8,128)}, f32[512,512]{1,0:T(8,128)}, f32[512,1536]{1,0:T(8,128)}, f32[512,512]{1,0:T(8,128)}, f32[512,2048]{1,0:T(8,128)}, /*index=5*/f32[2048,512]{1,0:T(8,128)}) async-done(((f32[512,1536]{1,0:T(8,128)}, f32[512,512]{1,0:T(8,128)}, f32[512,1536]{1,0:T(8,128)}, f32[512,512]{1,0:T(8,128)}, f32[512,2048]{1,0:T(8,128)}, ...) | async-done | bytes 16777232 | tf_op jit(solution)/shard_map/psum | solution.py:273
  877.0 3.9 copy.199
  (241 shorter events, 106.7 us)
Async XLA Ops:
  7.2 195.4 %copy-start = (bf16[512,2048]{1,0:T(8,128)(2,1)S(1)}, bf16[512,2048]{1,0:T(8,128)(2,1)}, u32[]{:S(2)}) copy-start(bf16[512,2048]{1,0:T(8,128)(2,1)} %param.34) | copy-start | bytes 6291460
  7.2 5.2 copy-start.17
  7.2 117.8 %all-gather.6.cloned.1.call-start = ((), (), s32[]{:S(2)}) async-start(), calls=%async_computation | async-start | bytes 3932160 | tf_op jit(solution)/shard_map/all_gather | solution.py:115
  10.5 3.9 copy-start.54
  10.5 3.9 copy-start.55
  10.5 3.9 copy-start.56
  10.5 3.9 copy-start.57
  14.4 9.7 %copy-start.49 = (f32[512]{0:T(512)}, f32[512]{0:T(512)S(1)}, u32[]{:S(2)}) copy-start(f32[512]{0:T(512)S(1)} %convert_element_type.126) | copy-start | bytes 6148
  14.4 9.7 %copy-start.52 = (f32[512]{0:T(512)}, f32[512]{0:T(512)S(1)}, u32[]{:S(2)}) copy-start(f32[512]{0:T(512)S(1)} %convert_element_type.127) | copy-start | bytes 6148
  15.1 9.1 %copy-start.43 = (f32[768]{0:T(1024)}, f32[768]{0:T(1024)S(1)}, u32[]{:S(2)}) copy-start(f32[768]{0:T(1024)S(1)} %add.144) | copy-start | bytes 9220
  15.1 9.0 %copy-start.47 = (f32[768]{0:T(1024)}, f32[768]{0:T(1024)S(1)}, u32[]{:S(2)}) copy-start(f32[768]{0:T(1024)S(1)} %rsqrt.33) | copy-start | bytes 9220
  15.3 8.8 copy-start.45
  32.9 6.9 copy-start.34
  58.7 130.6 %all-gather.8.cloned.1.call-start = ((), (), s32[]{:S(2)}) async-start(), calls=%async_computation.1 | async-start | bytes 3932160 | tf_op jit(solution)/shard_map/all_gather | solution.py:116
  60.9 496.1 %all-reduce.6.cloned.1.call-start = ((), (), s32[]{:S(2)}) async-start(), calls=%async_computation.2 | async-start | bytes 16777216
  128.9 4.7 copy-start.2
  202.3 13.1 %copy-start.6 = (f32[768,512]{1,0:T(8,128)}, f32[768,512]{1,0:T(8,128)S(1)}, u32[]{:S(2)}) copy-start(f32[768,512]{1,0:T(8,128)S(1)} %get-tuple-element.115) | copy-start | bytes 4718596
  202.6 4.8 copy-start.18
  202.6 4.8 copy-start.62
  223.1 10.9 %slice-start = ((s8[12582912]{0:T(1024)(128)(4,1)}), s8[4194304]{0:T(1024)(128)(4,1)S(1)}, s32[]{:S(2)}) async-start(s8[12582912]{0:T(1024)(128)(4,1)} %bitcast.136), calls=%async_computation.4 | async-start | bytes 8388608
  224.8 9.1 %slice-start.1 = ((s8[12582912]{0:T(1024)(128)(4,1)}), s8[4194304]{0:T(1024)(128)(4,1)S(1)}, s32[]{:S(2)}) async-start(s8[12582912]{0:T(1024)(128)(4,1)} %bitcast.136), calls=%async_computation.5 | async-start | bytes 8388608
  224.8 9.1 %slice-start.2 = ((s8[12582912]{0:T(1024)(128)(4,1)}), s8[4194304]{0:T(1024)(128)(4,1)S(1)}, s32[]{:S(2)}) async-start(s8[12582912]{0:T(1024)(128)(4,1)} %bitcast.136), calls=%async_computation.6 | async-start | bytes 8388608
  267.8 609.1 %all-reduce.8.cloned.1.call-start = ((), (), s32[]{:S(2)}) async-start(), calls=%async_computation.3 | async-start | bytes 33554432 | tf_op jit(solution)/shard_map/psum | solution.py:273
  278.0 5.0 copy-start.19
  278.0 5.0 copy-start.66
  283.0 3.9 copy-start.7
  283.0 3.9 copy-start.29
  604.5 4.0 copy-start.44
  604.5 4.1 copy-start.14
  877.0 3.9 copy-start.33
  877.0 4.9 copy-start.27
  881.8 4.0 copy-start.24
  (42 other events, 97.8 us)
Sparse Core Ops, SparseCore 0:
  58.8 66.1 all-gather.5
  127.1 62.0 all-gather.7
  268.0 289.0 all-reduce.5
  594.2 282.7 all-reduce.7
where the time goes:
time: 904 us; the launch traced here: 900 us
  waiting for transfers between devices  586 us (65%)
  matrix products  115 us (13%)
  local copies, waits for them, and re-layouts  104 us (12%)
  blocking collectives  54.1 us (6%)
  other arithmetic  24.5 us (3%)
  between operations  15.8 us (2%)
    unnamed x5, waiting for transfers between devices  266 us
    psum x1, waiting for transfers between devices, per_device(): lax.psum((g_miss, g_gain_one, g_shift_one, g_feat_qkv, g_feat_out, g_gain...  220 us
    all_gather x1, waiting for transfers between devices, per_device(): values_piece = lax.all_gather(row_values, 'blk', axis=0, tiled=True)  55.6 us
    all_gather x1, waiting for transfers between devices, per_device(): keys_piece = lax.all_gather(row_keys, 'blk', axis=0, tiled=True)  44.7 us
    psum x1, blocking collectives, per_device(): lax.psum((g_miss, g_gain_one, g_shift_one, g_feat_qkv, g_feat_out, g_gain...  41.2 us
    unnamed x157, local copies, waits for them, and re-layouts  40 us
    dot_general x6, matrix products, matmul_plain(): return jnp.dot(left, right, preferred_element_type=jnp.float32)  20.8 us
    dot_general x6, matrix products, matmul_left_t(): lax.dot_general(left, right, (((0,), (0,)), ((), ())), preferred_element_...  18.8 us
  transfers between devices with their start and end apart: 4, of which 4 were waited for; matrix products, arithmetic and copies ran while one was open for 6% of the time, Pallas kernels for 0%

commit v1 on v0

v1 whole, which is shorter than its diff:
```python
import functools
import math

import jax
import jax.numpy as jnp
from jax import lax
from jax.experimental import pallas as pl
from jax.experimental.pallas import tpu as pltpu
from jax.sharding import PartitionSpec as P

HEADS = 4
HEAD = 128
EPS = 1e-05
SCALE = 1.0 / math.sqrt(HEAD)
MESH = pl.DeviceIdType.MESH
F32 = jnp.float32
BF16 = jnp.bfloat16
EMBED, GAIN1, SHIFT1, GAIN2, SHIFT2, GAIN3, SHIFT3, OUT_BIAS, IN_BIAS = range(9)
B_FF_OUT, B_FF_IN, B_ROW_OUT, B_ROW_QKV, B_FEAT_OUT, B_FEAT_QKV = 0, 4, 8, 9, 12, 13
BLOCKS = 16
CHUNK = 64


def dot(a, b):
    return jnp.dot(a, b, preferred_element_type=F32)


def dot_rt(a, b):
    return lax.dot_general(a, b, (((1,), (1,)), ((), ())), preferred_element_type=F32)


def dot_lt(a, b):
    return lax.dot_general(a, b, (((0,), (0,)), ((), ())), preferred_element_type=F32)


def stats(x):
    center = x - jnp.mean(x, axis=-1, keepdims=True)
    rstd = lax.rsqrt(jnp.mean(center * center, axis=-1, keepdims=True) + EPS)
    return center * rstd, rstd


def norm_back(x, gain, dy):
    xhat, rstd = stats(x)
    dxh = dy * gain
    dx = rstd * (
        dxh
        - jnp.mean(dxh, axis=-1, keepdims=True)
        - xhat * jnp.mean(dxh * xhat, axis=-1, keepdims=True)
    )
    dgain = jnp.sum(dy * xhat, axis=0, keepdims=True)
    dshift = jnp.sum(dy, axis=0, keepdims=True)
    return dx, dgain, dshift


def layer_kernel(
    nb,
    cells_h,
    cot_h,
    absent,
    ctx,
    vec,
    wfqkv_h,
    wfout_h,
    wrqkv_h,
    wrout_h,
    wfin_h,
    wfdn_h,
    act_h,
    igrad_h,
    grads_h,
    gvec,
    cells,
    cot,
    wfqkv,
    wfout,
    wrqkv,
    wrout,
    wfin,
    wfdn,
    wkvt,
    af,
    n1,
    fqkv,
    fp,
    fo,
    n2,
    rss,
    rsr,
    g2,
    hid,
    gin,
    n3,
    ro,
    gy2,
    accq,
    ctxa,
    act,
    dn2,
    load_sem,
    out_sem,
    ctx_send,
    ctx_recv,
    ag_send,
    ag_recv,
    fwd_send,
    rs_send,
    rs_recv,
):
    cols, rows, width = cells.shape
    seg = width
    ff_blocks = wfdn.shape[0] // seg
    t = lax.axis_index("tab")
    z = lax.axis_index("blk")

    loads = [
        pltpu.make_async_copy(src, dst, load_sem.at[i])
        for i, (src, dst) in enumerate(
            [
                (cells_h, cells),
                (wfqkv_h, wfqkv),
                (wfout_h, wfout),
                (wrqkv_h, wrqkv),
                (wrout_h, wrout),
                (wfin_h, wfin),
                (wfdn_h, wfdn),
                (cot_h, cot),
            ]
        )
    ]
    for load in loads:
        load.start()

    barrier = pltpu.get_barrier_semaphore()
    for d in range(1, nb):
        pl.semaphore_signal(
            barrier, inc=1, device_id=(t, lax.rem(z + d, nb)), device_id_type=MESH
        )
    pl.semaphore_wait(barrier, nb - 1)

    ctxa[z] = ctx[...]
    ctx_copies = [
        pltpu.make_async_remote_copy(
            src_ref=ctxa.at[z],
            dst_ref=ctxa.at[z],
            send_sem=ctx_send.at[d],
            recv_sem=ctx_recv.at[z],
            device_id=(t, lax.rem(z + d, nb)),
            device_id_type=MESH,
        )
        for d in range(1, nb)
    ]
    for copy in ctx_copies:
        copy.start()

    def own_send(c, d):
        return pltpu.make_async_remote_copy(
            src_ref=n2.at[c, z],
            dst_ref=n2.at[c, z],
            send_sem=ag_send.at[c, d + 2],
            recv_sem=ag_recv.at[c, z],
            device_id=(t, z + d),
            device_id_type=MESH,
        )

    def each_near(act_on):
        for d in (-1, 1, -2, 2):

            @pl.when(jnp.logical_and(z + d >= 0, z + d < nb))
            def _():
                act_on(d)

    def start_gather(c):
        each_near(lambda d: own_send(c, d).start())

    def forward(c, far):
        return pltpu.make_async_remote_copy(
            src_ref=n2.at[c, far],
            dst_ref=n2.at[c, far],
            send_sem=fwd_send.at[c],
            recv_sem=ag_recv.at[c, far],
            device_id=(t, nb - 1 - far),
            device_id_type=MESH,
        )

    def await_block(c, s):
        pltpu.make_async_copy(n2.at[c, s], n2.at[c, s], ag_recv.at[c, s]).wait()

    def at_middle(run):
        for mid in (1, nb - 2):

            @pl.when(z == mid)
            def _():
                run(nb - 1 if mid == 1 else 0)

    def start_forward(c):
        def go(far):
            await_block(c, far)
            forward(c, far).start()

        at_middle(go)

    def await_gather(c):
        for s in range(nb):
            skip = z == s
            if s == 0:
                skip = jnp.logical_or(skip, z == nb - 2)
            if s == nb - 1:
                skip = jnp.logical_or(skip, z == 1)

            @pl.when(jnp.logical_not(skip))
            def _():
                await_block(c, s)

    def row(i):
        return vec[i : i + 1, :]

    def base_of(c, r):
        return jnp.where(
            absent[c, pl.ds(r, CHUNK), :] > 0, row(EMBED), cells[c, pl.ds(r, CHUNK), :].astype(F32)
        )

    ones = (
        lax.broadcasted_iota(jnp.int32, (width, HEAD), 0) // HEAD
        == lax.broadcasted_iota(jnp.int32, (width, HEAD), 1)
    ).astype(BF16)
    ones_t = (
        lax.broadcasted_iota(jnp.int32, (HEAD, width), 1) // HEAD
        == lax.broadcasted_iota(jnp.int32, (HEAD, width), 0)
    ).astype(BF16)

    gvec[...] = jnp.zeros_like(gvec)
    loads[0].wait()
    for c in range(cols):
        for r in range(0, rows, CHUNK):
            xhat, _ = stats(base_of(c, r))
            n1[c, pl.ds(r, CHUNK), :] = (xhat * row(GAIN1) + row(SHIFT1)).astype(BF16)
    loads[1].wait()
    n1_all = n1[...].reshape(cols * rows, width)
    for b in range(3):
        fqkv[b] = (
            dot(n1_all, wfqkv[:, b * seg : (b + 1) * seg]).astype(BF16).reshape(cols, rows, width)
        )

    def feature_forward(hi, lo, spread):
        for i in range(cols):
            for j in range(cols):
                for r in range(0, rows, CHUNK):
                    prod = fqkv[0, i, pl.ds(r, CHUNK), :].astype(F32) * fqkv[
                        1, j, pl.ds(r, CHUNK), :
                    ].astype(F32)
                    top = prod.astype(BF16)
                    hi[pl.ds(j * rows + r, CHUNK), :] = top
                    lo[pl.ds(j * rows + r, CHUNK), :] = (prod - top.astype(F32)).astype(BF16)
            scores = (dot(hi[...], ones) + dot(lo[...], ones)) * SCALE
            parts = [scores[j * rows : (j + 1) * rows] for j in range(cols)]
            top = functools.reduce(jnp.maximum, parts)
            parts = [jnp.exp(part - top) for part in parts]
            inv = 1.0 / functools.reduce(jnp.add, parts)
            for j in range(cols):
                fp[i, j] = parts[j] * inv
            spread[...] = dot(
                fp[i].reshape(cols * rows, HEAD).astype(BF16), ones_t
            )
            for r in range(0, rows, CHUNK):
                total = functools.reduce(
                    jnp.add,
                    [
                        spread[pl.ds(j * rows + r, CHUNK), :]
                        * fqkv[2, j, pl.ds(r, CHUNK), :].astype(F32)
                        for j in range(cols)
                    ],
                )
                fo[i, pl.ds(r, CHUNK), :] = total.astype(BF16)
            if i == 0:
                loads[2].wait()
            spread[0:rows, :] = dot(fo[i], wfout[...])
            for r in range(0, rows, CHUNK):
                after = base_of(i, r) + spread[pl.ds(r, CHUNK), :]
                af[i, pl.ds(r, CHUNK), :] = after
                xhat, _ = stats(after)
                n2[i, z, pl.ds(r, CHUNK), :] = (xhat * row(GAIN2) + row(SHIFT2)).astype(BF16)
            if i == 0:
                start_gather(0)

    pl.run_scoped(
        feature_forward,
        pltpu.VMEM((cols * rows, width), BF16),
        pltpu.VMEM((cols * rows, width), BF16),
        pltpu.VMEM((cols * rows, width), F32),
    )

    loads[3].wait()
    for b in range(2):
        wkvt[b] = (
            wrqkv[:, (b + 1) * seg : (b + 2) * seg].astype(F32).T.astype(BF16)
        )
    for load in loads[4:]:
        load.wait()
    for s in range(nb):

        @pl.when(z != s)
        def _():
            pltpu.make_async_copy(ctxa.at[s], ctxa.at[s], ctx_recv.at[s]).wait()

    accq[...] = jnp.zeros_like(accq)

    def rs_copy(c, owner, dest, slot, k):
        return pltpu.make_async_remote_copy(
            src_ref=rss.at[c, owner],
            dst_ref=rsr.at[c, slot],
            send_sem=rs_send.at[c, k],
            recv_sem=rs_recv.at[c, slot],
            device_id=(t, dest),
            device_id_type=MESH,
        )

    def rs_plan(me):
        plan = []
        for owner in range(nb):
            distance = abs(owner - me)
            if distance == 0 or (distance == 2 and 0 < me < nb - 1 and owner in (0, nb - 1)):
                continue
            if distance == 3:
                dest = 1 if me == 0 else nb - 2
                plan.insert(0, (owner, dest, dest))
            else:
                plan.append((owner, owner, me))
        return plan

    def start_scatter(c):
        for me in range(nb):

            @pl.when(z == me)
            def _():
                for k, (owner, dest, slot) in enumerate(rs_plan(me)):
                    rs_copy(c, owner, dest, slot, k).start()

    def await_slot(c, s):
        pltpu.make_async_copy(rsr.at[c, s], rsr.at[c, s], rs_recv.at[c, s]).wait()

    def combine(c):
        for me in (1, nb - 2):

            @pl.when(z == me)
            def _():
                owner = nb - 1 if me == 1 else 0
                await_slot(c, me)
                rss[c, owner] = (
                    rss[c, owner].astype(F32) + rsr[c, me].astype(F32)
                ).astype(BF16)
                rs_copy(c, owner, owner, me, 3).start()

    def columns_stage(bias, q, kv, kvt, dkv, p, ot, dgel, ar, dq):
        for s in range(nb):
            b = (ctxa[s].astype(F32) - 1.0) * 1e30
            for lane in range(0, rows, HEAD):
                bias[pl.ds(s * rows, rows), lane : lane + HEAD] = b

        def column(c, _):
            start_forward(c)

            @pl.when(c + 1 < cols)
            def _():
                start_gather(c + 1)

            await_gather(c)
            x = n2[c].reshape(nb * rows, width)
            own = n2[c, z]
            q[...] = dot(own, wrqkv[:, 0:seg]).astype(BF16)
            kv[0] = dot(x, wrqkv[:, seg : 2 * seg]).astype(BF16)
            kvt[1] = dot_rt(wkvt[1], x).astype(BF16)
            for h in range(HEADS):
                hs = slice(h * HEAD, (h + 1) * HEAD)
                s = dot_rt(kv[0, :, hs], q[:, hs]) + bias[...]
                top = jnp.max(s, axis=0, keepdims=True)
                e = jnp.exp((s - top) * SCALE)
                p[h] = (e * (1.0 / jnp.sum(e, axis=0, keepdims=True))).astype(BF16)
                ot[hs, :] = dot(kvt[1, hs, :], p[h])
            ro[c] = ot[...].T.astype(BF16)
            kv[1] = dot(x, wrqkv[:, 2 * seg : 3 * seg]).astype(BF16)
            kvt[0] = dot_rt(wkvt[0], x).astype(BF16)

            ar[...] = dot(ro[c], wrout[...])
            for r in range(0, rows, CHUNK):
                rr = pl.ds(r, CHUNK)
                after = af[c, rr, :] + ar[rr, :]
                ar[rr, :] = after
                xhat, _ = stats(after)
                n3[c, rr, :] = (xhat * row(GAIN3) + row(SHIFT3)).astype(BF16)
            for f in range(ff_blocks):
                fs = slice(f * seg, (f + 1) * seg)
                dgel[f] = dot(n3[c], wfin[:, fs])
                for r in range(0, rows, CHUNK):
                    rr = pl.ds(r, CHUNK)
                    u = dgel[f, rr, :] + row(IN_BIAS + f)
                    c0 = math.sqrt(2.0 / math.pi)
                    sq = u * u
                    th = jnp.tanh(u * (c0 + (c0 * 0.044715) * sq))
                    half = 0.5 * (1.0 + th)
                    hid[c, rr, fs] = (u * half).astype(BF16)
                    dgel[f, rr, :] = half + 0.5 * u * (1.0 - th * th) * (
                        c0 + (3.0 * c0 * 0.044715) * sq
                    )
            act[c] = (ar[...] + dot(hid[c], wfdn[...]) + row(OUT_BIAS)).astype(BF16)
            pltpu.make_async_copy(act.at[c], act_h.at[c], out_sem.at[c]).start()
            for f in range(ff_blocks):
                fs = slice(f * seg, (f + 1) * seg)
                gi = (dot_rt(cot[c], wfdn[fs, :]) * dgel[f]).astype(BF16)
                gin[c, :, fs] = gi
                gvec[IN_BIAS + f : IN_BIAS + f + 1, :] += jnp.sum(
                    gi.astype(F32), axis=0, keepdims=True
                )
            dgel[0] = dot_rt(gin[c], wfin[...])
            for r in range(0, rows, CHUNK):
                rr = pl.ds(r, CHUNK)
                dx, dgain, dshift = norm_back(ar[rr, :], row(GAIN3), dgel[0, rr, :])
                g3 = cot[c, rr, :].astype(F32)
                g = g3 + dx
                g2[c, rr, :] = g
                gy2[c, rr, :] = g.astype(BF16)
                gvec[GAIN3 : GAIN3 + 1, :] += dgain
                gvec[SHIFT3 : SHIFT3 + 1, :] += dshift
                gvec[OUT_BIAS : OUT_BIAS + 1, :] += jnp.sum(g3, axis=0, keepdims=True)
            ar[...] = dot_rt(gy2[c], wrout[...])
            gro = ar[...].astype(BF16)
            for h in range(HEADS):
                hs = slice(h * HEAD, (h + 1) * HEAD)
                dp = dot_rt(kv[1, :, hs], gro[:, hs])
                pr = p[h].astype(F32)
                ds = (pr * (dp - jnp.sum(pr * dp, axis=0, keepdims=True))).astype(BF16)
                dkv[0, :, hs] = (dot(ds, q[:, hs]) * SCALE).astype(BF16)
                dkv[1, :, hs] = dot(p[h], gro[:, hs]).astype(BF16)
                ot[hs, :] = dot(kvt[0, hs, :], ds)
            dq[...] = (ot[...].T * SCALE).astype(BF16)
            for o in range(nb):
                os = slice(o * rows, (o + 1) * rows)
                rss[c, o] = (
                    dot_rt(dkv[0, os, :], wrqkv[:, seg : 2 * seg])
                    + dot_rt(dkv[1, os, :], wrqkv[:, 2 * seg : 3 * seg])
                ).astype(BF16)
            start_scatter(c)

            @pl.when(c > 0)
            def _():
                combine(c - 1)

            af_part = dot_rt(dq[...], wrqkv[:, 0:seg])
            dn2[c] = af_part
            accq[0] += dot_lt(own, dq[...])
            accq[1] += dot_lt(x, dkv[0])
            accq[2] += dot_lt(x, dkv[1])
            return 0

        lax.fori_loop(0, cols, column, 0)

    pl.run_scoped(
        columns_stage,
        pltpu.VMEM((nb * rows, rows), F32),
        pltpu.VMEM((rows, width), BF16),
        pltpu.VMEM((2, nb * rows, width), BF16),
        pltpu.VMEM((2, width, nb * rows), BF16),
        pltpu.VMEM((2, nb * rows, width), BF16),
        pltpu.VMEM((HEADS, nb * rows, rows), BF16),
        pltpu.VMEM((width, rows), F32),
        pltpu.VMEM((ff_blocks, rows, width), F32),
        pltpu.VMEM((rows, width), F32),
        pltpu.VMEM((rows, width), BF16),
    )

    def weights_stage(gb):
        def flat(ref):
            return ref[...].reshape(cols * rows, ref.shape[-1])

        for f in range(ff_blocks):
            fs = slice(f * seg, (f + 1) * seg)
            gb[B_FF_OUT + f] = dot_lt(hid[:, :, fs].reshape(cols * rows, seg), flat(cot)).astype(BF16)
            gb[B_FF_IN + f] = dot_lt(flat(n3), gin[:, :, fs].reshape(cols * rows, seg)).astype(BF16)
        gb[B_ROW_OUT] = dot_lt(flat(ro), flat(gy2)).astype(BF16)
        for b in range(3):
            gb[B_ROW_QKV + b] = accq[b].astype(BF16)

    def weigh(spread, source, part, dest, dest_part, i, scale):
        for r in range(0, rows, CHUNK):
            rr = pl.ds(r, CHUNK)
            total = functools.reduce(
                jnp.add,
                [
                    spread[pl.ds(j * rows + r, CHUNK), :]
                    * (source[j, rr, :] if part is None else source[part, j, rr, :]).astype(F32)
                    for j in range(cols)
                ],
            )
            dest[dest_part, i, rr, :] = (total * scale).astype(BF16)

    def feature_backward(gb, hi, lo, spread, gfo, dqkv, dsl):
        for c in range(cols):
            for s in range(nb):
                skip = z == s
                if s in (0, nb - 1):
                    skip = jnp.logical_or(skip, z == nb - 1 - s)

                @pl.when(jnp.logical_not(skip))
                def _():
                    await_slot(c, s)
                    dn2[c] += rsr[c, s].astype(F32)

            for r in range(0, rows, CHUNK):
                rr = pl.ds(r, CHUNK)
                dy = dn2[c, rr, :] + rss[c, z, rr, :].astype(F32)
                dx, dgain, dshift = norm_back(af[c, rr, :], row(GAIN2), dy)
                g = g2[c, rr, :] + dx
                g2[c, rr, :] = g
                gy2[c, rr, :] = g.astype(BF16)
                gvec[GAIN2 : GAIN2 + 1, :] += dgain
                gvec[SHIFT2 : SHIFT2 + 1, :] += dshift
        gy1 = gy2[...].reshape(cols * rows, width)
        gfo[...] = dot_rt(gy1, wfout[...]).astype(BF16).reshape(cols, rows, width)
        gb[B_FEAT_OUT] = dot_lt(fo[...].reshape(cols * rows, width), gy1).astype(BF16)
        for i in range(cols):
            for j in range(cols):
                for r in range(0, rows, CHUNK):
                    prod = gfo[i, pl.ds(r, CHUNK), :].astype(F32) * fqkv[
                        2, j, pl.ds(r, CHUNK), :
                    ].astype(F32)
                    top = prod.astype(BF16)
                    hi[pl.ds(j * rows + r, CHUNK), :] = top
                    lo[pl.ds(j * rows + r, CHUNK), :] = (prod - top.astype(F32)).astype(BF16)
            dp = dot(hi[...], ones) + dot(lo[...], ones)
            parts = [dp[j * rows : (j + 1) * rows] for j in range(cols)]
            mean = functools.reduce(jnp.add, [fp[i, j] * parts[j] for j in range(cols)])
            for j in range(cols):
                dsl[i, j] = (fp[i, j] * (parts[j] - mean)).astype(BF16)
        for i in range(cols):
            spread[...] = dot(dsl[i].reshape(cols * rows, HEAD), ones_t)
            weigh(spread, fqkv, 1, dqkv, 0, i, SCALE)
            spread[...] = dot(jnp.concatenate([dsl[j, i] for j in range(cols)], axis=0), ones_t)
            weigh(spread, fqkv, 0, dqkv, 1, i, SCALE)
            spread[...] = dot(
                jnp.concatenate([fp[j, i].astype(BF16) for j in range(cols)], axis=0), ones_t
            )
            weigh(spread, gfo, None, dqkv, 2, i, 1.0)
        n1_flat = n1[...].reshape(cols * rows, width)
        for b in range(3):
            gb[B_FEAT_QKV + b] = dot_lt(
                n1_flat, dqkv[b].reshape(cols * rows, width)
            ).astype(BF16)
        spread[...] = functools.reduce(
            jnp.add,
            [
                dot_rt(
                    dqkv[b].reshape(cols * rows, width), wfqkv[:, b * seg : (b + 1) * seg]
                )
                for b in range(3)
            ],
        )
        for c in range(cols):
            for r in range(0, rows, CHUNK):
                rr = pl.ds(r, CHUNK)
                dx, dgain, dshift = norm_back(
                    base_of(c, r), row(GAIN1), spread[pl.ds(c * rows + r, CHUNK), :]
                )
                g = g2[c, rr, :] + dx
                gone = absent[c, rr, :] > 0
                g2[c, rr, :] = jnp.where(gone, 0.0, g)
                gvec[GAIN1 : GAIN1 + 1, :] += dgain
                gvec[SHIFT1 : SHIFT1 + 1, :] += dshift
                gvec[EMBED : EMBED + 1, :] += jnp.sum(
                    jnp.where(gone, g, 0.0), axis=0, keepdims=True
                )

    def tail_stage(gb):
        weights_stage(gb)
        combine(cols - 1)
        pl.run_scoped(
            functools.partial(feature_backward, gb),
            pltpu.VMEM((cols * rows, width), BF16),
            pltpu.VMEM((cols * rows, width), BF16),
            pltpu.VMEM((cols * rows, width), F32),
            pltpu.VMEM((cols, rows, width), BF16),
            pltpu.VMEM((3, cols, rows, width), BF16),
            pltpu.VMEM((cols, cols, rows, HEAD), BF16),
        )
        grads_copy = pltpu.make_async_copy(gb, grads_h, out_sem.at[cols + 1])
        grads_copy.start()
        grads_copy.wait()

    pl.run_scoped(tail_stage, pltpu.VMEM((BLOCKS, width, width), BF16))

    igrad_copy = pltpu.make_async_copy(g2, igrad_h, out_sem.at[cols])
    igrad_copy.start()
    for c in range(cols):
        pltpu.make_async_copy(act.at[c], act_h.at[c], out_sem.at[c]).wait()
        each_near(lambda d: own_send(c, d).wait_send())
        at_middle(lambda far: forward(c, far).wait_send())
        for me in range(nb):

            @pl.when(z == me)
            def _():
                plan = rs_plan(me)
                for k, (owner, dest, slot) in enumerate(plan):
                    rs_copy(c, owner, dest, slot, k).wait_send()
                if 0 < me < nb - 1:
                    owner = nb - 1 if me == 1 else 0
                    rs_copy(c, owner, owner, me, 3).wait_send()

    for copy in ctx_copies:
        copy.wait_send()
    igrad_copy.wait()


def per_device(
    cells,
    missing,
    context,
    cotangent,
    miss_embed,
    norm1_gain,
    norm1_shift,
    feat_qkv,
    feat_out,
    norm2_gain,
    norm2_shift,
    row_qkv,
    row_out,
    norm3_gain,
    norm3_shift,
    ff_in,
    ff_in_bias,
    ff_out,
    ff_out_bias,
):
    _, rows, cols, width = cells.shape
    nb = lax.axis_size("blk")
    ff = ff_in.shape[1]
    ff_blocks = ff // width

    cells_t = jnp.transpose(cells[0], (1, 0, 2))
    cot_t = jnp.transpose(cotangent[0], (1, 0, 2))
    absent = jnp.transpose(missing[0], (1, 0))[:, :, None].astype(F32)
    ctx = jnp.broadcast_to(context[0][:, None].astype(BF16), (rows, HEAD))
    vec = jnp.concatenate(
        [
            jnp.stack(
                [
                    miss_embed,
                    norm1_gain,
                    norm1_shift,
                    norm2_gain,
                    norm2_shift,
                    norm3_gain,
                    norm3_shift,
                    ff_out_bias,
                ]
            ),
            ff_in_bias.reshape(ff_blocks, width),
            jnp.zeros((8 - ff_blocks, width), BF16),
        ]
    ).astype(F32)

    any_spec = pl.BlockSpec(memory_space=pl.ANY)
    vmem_spec = pl.BlockSpec(memory_space=pltpu.VMEM)
    token = (cols, rows, width)
    vm = pltpu.VMEM
    act, igrad, grads, gvec = pl.pallas_call(
        functools.partial(layer_kernel, nb),
        out_shape=(
            jax.ShapeDtypeStruct(token, BF16),
            jax.ShapeDtypeStruct(token, F32),
            jax.ShapeDtypeStruct((BLOCKS, width, width), BF16),
            jax.ShapeDtypeStruct((16, width), F32),
        ),
        in_specs=[any_spec] * 2 + [vmem_spec] * 3 + [any_spec] * 6,
        out_specs=(any_spec, any_spec, any_spec, vmem_spec),
        scratch_shapes=[
            vm(token, BF16),
            vm(token, BF16),
            vm(feat_qkv.shape, BF16),
            vm(feat_out.shape, BF16),
            vm(row_qkv.shape, BF16),
            vm(row_out.shape, BF16),
            vm(ff_in.shape, BF16),
            vm(ff_out.shape, BF16),
            vm((2, width, width), BF16),
            vm(token, F32),
            vm(token, BF16),
            vm((3,) + token, BF16),
            vm((cols, cols, rows, HEAD), F32),
            vm(token, BF16),
            vm((cols, nb, rows, width), BF16),
            vm((cols, nb, rows, width), BF16),
            vm((cols, nb, rows, width), BF16),
            vm(token, F32),
            vm((cols, rows, ff), BF16),
            vm((cols, rows, ff), BF16),
            vm(token, BF16),
            vm(token, BF16),
            vm(token, BF16),
            vm((3, width, width), F32),
            vm((nb, rows, HEAD), BF16),
            vm(token, BF16),
            vm(token, F32),
            pltpu.SemaphoreType.DMA((8,)),
            pltpu.SemaphoreType.DMA((cols + 2,)),
            pltpu.SemaphoreType.DMA((nb,)),
            pltpu.SemaphoreType.DMA((nb,)),
            pltpu.SemaphoreType.DMA((cols, 5)),
            pltpu.SemaphoreType.DMA((cols, nb)),
            pltpu.SemaphoreType.DMA((cols,)),
            pltpu.SemaphoreType.DMA((cols, nb)),
            pltpu.SemaphoreType.DMA((cols, nb)),
        ],
        compiler_params=pltpu.CompilerParams(
            collective_id=0, has_side_effects=True, vmem_limit_bytes=64 * 1024 * 1024
        ),
    )(
        cells_t,
        cot_t,
        absent,
        ctx,
        vec,
        feat_qkv,
        feat_out,
        row_qkv,
        row_out,
        ff_in,
        ff_out,
    )
    grads, gvec = lax.psum((grads.astype(F32), gvec), ("tab", "blk"))

    def side(first, count):
        return jnp.concatenate([grads[first + b] for b in range(count)], axis=1)

    return (
        jnp.transpose(act, (1, 0, 2))[None],
        jnp.transpose(igrad, (1, 0, 2))[None],
        gvec[EMBED],
        gvec[GAIN1],
        gvec[SHIFT1],
        side(B_FEAT_QKV, 3),
        grads[B_FEAT_OUT],
        gvec[GAIN2],
        gvec[SHIFT2],
        side(B_ROW_QKV, 3),
        grads[B_ROW_OUT],
        gvec[GAIN3],
        gvec[SHIFT3],
        side(B_FF_IN, ff_blocks),
        gvec[IN_BIAS : IN_BIAS + ff_blocks].reshape(ff),
        grads[B_FF_OUT : B_FF_OUT + ff_blocks].reshape(ff, width),
        gvec[OUT_BIAS],
    )


def solution(mesh):
    split = (
        P("tab", "blk", None, None),
        P("tab", "blk", None),
        P("tab", "blk"),
        P("tab", "blk", None, None),
    )
    return jax.shard_map(
        per_device,
        mesh=mesh,
        in_specs=split + (P(),) * 15,
        out_specs=(P("tab", "blk", None, None),) * 2 + (P(),) * 15,
        check_vma=False,
    )
```

time: 904 us -> 454 us (0.50)
  waiting for transfers between devices: 586 us -> 0 us
  blocking collectives: 54.1 us -> 279 us
  Pallas kernels: 0 us -> 135 us
  matrix products: 115 us -> 0 us
  local copies, waits for them, and re-layouts: 104 us -> 23.8 us
  other arithmetic: 24.5 us -> 9.77 us
  between operations: 15.8 us -> 1.12 us
    unnamed x5 -> x0, waiting for transfers between devices: 266 us -> none
    psum x1, blocking collectives: 41.2 us -> 279 us  [per_device(): grads, gvec = lax.psum((grads.astype(F32), gvec), ('tab', 'blk'))]
    psum x1 -> x0, waiting for transfers between devices: 220 us -> none  [per_device(): lax.psum((g_miss, g_gain_one, g_shift_one, g_feat_qkv, g_feat_out, g_gain...]
    pallas_call x0 -> x1, Pallas kernels: none -> 135 us  [per_device(): pl.pallas_call(functools.partial(layer_kernel, nb), out_shape=(jax.ShapeD...]
    dot_general x29 -> x0, matrix products: 108 us -> none  [the longest x6 20.8 us: matmul_plain(): return jnp.dot(left, right, preferred_element_type=jnp.float32)]
    all_gather x2 -> x0, waiting for transfers between devices: 100 us -> none  [the longest x1 55.6 us: per_device(): values_piece = lax.all_gather(row_values, 'blk', axis=0, tiled=True)]
    reshape x10 -> x1, local copies, waits for them, and re-layouts: 39.1 us -> 0.7 us  [per_device(): ff_in_bias.reshape(ff_blocks, width)]
    unnamed x157 -> x9, local copies, waits for them, and re-layouts: 40 us -> 2.64 us
  transfers between devices with their start and end apart: 4 -> 0, of which waited for: 4 -> 0; matrix products, arithmetic and copies ran while one was open for 6% -> 0% of each run, Pallas kernels for 0% -> 0%
where the time goes in v1:
time: 454 us; the launch traced here: 448 us
  blocking collectives  279 us (61%)
  Pallas kernels  135 us (30%)
  local copies, waits for them, and re-layouts  23.8 us (5%)
  other arithmetic  9.77 us (2%)
    psum x1, blocking collectives, per_device(): grads, gvec = lax.psum((grads.astype(F32), gvec), ('tab', 'blk'))  279 us
    pallas_call x1, Pallas kernels, per_device(): pl.pallas_call(functools.partial(layer_kernel, nb), out_shape=(jax.ShapeD...  135 us

profile of v1, /device:TPU:0, one launch (start us, length us, event | category | flops | bytes accessed | tf_op | source)
XLA Modules:
  0.0 448.3 jit_solution(13819754357683953794)
XLA Ops:
  0.7 0.7 convert_reduce_fusion
  1.4 0.7 stack.24
  2.0 0.7 stack.25
  2.7 0.7 stack.26
  3.4 0.7 stack.27
  4.1 0.7 stack.28
  4.8 0.7 stack.29
  5.4 0.7 stack.30
  6.1 0.7 stack.31
  6.8 0.7 convert_element_type.26
  7.5 0.7 reshape.53
  8.2 0.1 concatenate.12
  8.3 0.6 convert_element_type.32.vec
  8.9 0.7 broadcast_in_dim.15.ctx
  9.6 0.9 copy.37.absent
  10.6 135.0 %shard_map.314 = (bf16[3,256,512]{2,1,0:T(8,128)(2,1)}, f32[3,256,512]{2,1,0:T(8,128)}, bf16[16,512,512]{2,1,0:T(8,128)(2,1)}, f32[16,512]{1,0:T(8,128)}) custom-call(bf16[3,256,512]{2,1,0:T(8,128)(2,1)} %bitcast.57, bf16[3,256,512]{2,1,0:T(8,128)(2,1)} %bitcast.58, f32[3,256,1]{2,1,0:T(8,128)} %copy.37.absent, bf16[256,128]{1,0:T(8,128)(2,1)} %broadcast_in_dim.15.ctx, ...), custom_call_target="tpu_custom_call" | custom-call | tf_op jit(solution)/shard_map/pallas_call | solution.py:664
  145.6 278.6 %all-reduce.2 = (f32[16,512]{1,0:T(8,128)S(1)}, f32[16,512,512]{2,1,0:T(8,128)}) all-reduce(f32[16,512]{1,0:T(8,128)} %get-tuple-element.23, bf16[16,512,512]{2,1,0:T(8,128)(2,1)} %get-tuple-element.24), channel_id=1, replica_groups=mesh['tab'=8,'blk'=4] {'tab','blk'}, use_global_device_ids=true, to_apply=%region_0.0 | all-reduce | flops 4202496 | bytes 25231360 | tf_op jit(solution)/shard_map/psum | solution.py:728
  424.2 0.6 fusion
  424.8 0.6 copy.39
  425.4 4.6 %slice.108 = f32[4,512,512]{2,1,0:T(8,128)} slice(f32[16,512,512]{2,1,0:T(8,128)} %get-tuple-element.26), slice={[0:4], [0:512], [0:512]} | slice | bytes 8388608 | tf_op jit(solution)/shard_map/slice | solution.py:749
  430.0 8.1 %slice_bitcast_fusion.3 = (f32[512,512]{1,0:T(8,128)}, f32[512,512]{1,0:T(8,128)}, f32[512,512]{1,0:T(8,128)}, f32[512,512]{1,0:T(8,128)}, f32[512,512]{1,0:T(8,...) fusion(f32[16,512,512]{2,1,0:T(8,128)} %get-tuple-element.26), kind=kLoop, calls=%fused_computation.6 | loop fusion | bytes 25165824 | tf_op jit(solution)/shard_map/squeeze | solution.py:731
  438.1 4.6 %pad_maximum_fusion = f32[512,2048]{1,0:T(8,128)} fusion(f32[512,512]{1,0:T(8,128)} %get-tuple-element.28, f32[512,512]{1,0:T(8,128)} %get-tuple-element.29, f32[512,512]{1,0:T(8,128)} %get-tuple-element.30, f32[512,512]{1,0:T(8,128)} %get-tuple-element.27), kind=kLoop, calls=%fused_computation | loop fusion | flops 3145728 | bytes 8388608 | tf_op jit(solution)/shard_map/concatenate | solution.py:731
  442.7 0.0 copy-start.1
  442.7 0.0 copy-start
  442.7 3.1 pad_maximum_fusion.1
  445.8 0.0 copy-done.1
  445.8 0.9 copy.47
  446.7 0.0 copy-done
  446.7 1.1 copy.48
  (3 shorter events, 0.0 us)
Async XLA Ops:
  442.7 3.1 copy-start.1
  442.7 4.0 copy-start
